TPU v7x, 128 devices: a whole 4x4x4 slice. The times are simulated.
128 devices in a mesh: row: 16 (over z, y), col: 8 (over x, core).
Axes of the slice: x: 4, y: 4, z: 4, core: 2. Of those that a mesh axis runs over, the one named last changes fastest.
Arguments:
- image: bfloat16 [64, 64, 6144], P('row', None, 'col'), may hold values from -8 to 8
- filter_bank: float32 [2, 64, 64, 6144], P(None, None, 'row', 'col'), may hold values from -6 to 6
- gain_first: float32 [6144], P('col'), may hold values from 0.1 to 1.9
- gain_second: float32 [6144], P('col'), may hold values from 0.1 to 1.9
- w_in: bfloat16 [6144, 24576], P('col', 'row'), may hold values from -0.078125 to 0.078125
- b_in: float32 [24576], P('row'), may hold values from -4 to 4
- w_out: bfloat16 [24576, 6144], P('row', 'col'), may hold values from -0.0390625 to 0.0390625
- b_out: float32 [6144], P('col'), may hold values from -3 to 3
Outputs:
- block_out: bfloat16 [64, 64, 6144], P('row', None, 'col')
All inputs are finite; a program needn't handle non-finite values.
Results may differ from a plain program's by a relative error of at most 0.017.
Values may be sent and summed in bfloat16 or wider, within the bound.
No kernel may reach another device: no remote copies, remote signals or barrier semaphores. Data moves between devices by JAX's collectives and lax.ppermute only.
A program may use at most 128 MiB of HBM per device.

v0:
```python
import math
import jax
import jax.numpy as jnp
from jax import lax
from jax.sharding import PartitionSpec as P


def tables(count):
    index = jnp.arange(count, dtype=jnp.int32)
    angle = (index[:, None] * index[None, :] % count).astype(jnp.float32) * (2.0 * math.pi / count)
    return (jnp.cos(angle), jnp.sin(angle))


def finish_norm(values, totals, width_all):
    mean = totals[0][..., None] / width_all
    square = totals[1][..., None] / width_all
    return (values - mean) / jnp.sqrt(square - mean * mean + 1e-05)


def on_device(image, filter_bank, gain_first, gain_second, w_in, b_in, w_out, b_out):
    high = lax.Precision.HIGHEST
    rows_here, width, chans = image.shape
    height = rows_here * lax.axis_size("row")
    width_all = chans * lax.axis_size("col")
    source = image.astype(jnp.float32)
    totals = lax.psum((jnp.sum(source, axis=-1), jnp.sum(source * source, axis=-1)), "col")
    normed = finish_norm(source, totals, width_all) * gain_first
    cos_w, sin_w = tables(width)
    cos_h, sin_h = tables(height)
    col_re = jnp.einsum("rcd,ck->rkd", normed, cos_w, precision=high)
    col_im = -jnp.einsum("rcd,ck->rkd", normed, sin_w, precision=high)
    col_re, col_im = (
        lax.all_to_all(
            col_re.astype(jnp.bfloat16), "row", split_axis=1, concat_axis=0, tiled=True
        ).astype(col_re.dtype),
        lax.all_to_all(
            col_im.astype(jnp.bfloat16), "row", split_axis=1, concat_axis=0, tiled=True
        ).astype(col_im.dtype),
    )
    spec_re = jnp.einsum("rn,rkd->nkd", cos_h, col_re, precision=high) + jnp.einsum(
        "rn,rkd->nkd", sin_h, col_im, precision=high
    )
    spec_im = jnp.einsum("rn,rkd->nkd", cos_h, col_im, precision=high) - jnp.einsum(
        "rn,rkd->nkd", sin_h, col_re, precision=high
    )
    filt_re = filter_bank[0] * spec_re - filter_bank[1] * spec_im
    filt_im = filter_bank[0] * spec_im + filter_bank[1] * spec_re
    back_re = jnp.einsum("nr,nkd->rkd", cos_h, filt_re, precision=high) - jnp.einsum(
        "nr,nkd->rkd", sin_h, filt_im, precision=high
    )
    back_im = jnp.einsum("nr,nkd->rkd", sin_h, filt_re, precision=high) + jnp.einsum(
        "nr,nkd->rkd", cos_h, filt_im, precision=high
    )
    back_re, back_im = (
        lax.all_to_all(
            back_re.astype(jnp.bfloat16), "row", split_axis=0, concat_axis=1, tiled=True
        ).astype(back_re.dtype),
        lax.all_to_all(
            back_im.astype(jnp.bfloat16), "row", split_axis=0, concat_axis=1, tiled=True
        ).astype(back_im.dtype),
    )
    mixed = (
        jnp.einsum("rkd,kc->rcd", back_re, cos_w, precision=high)
        - jnp.einsum("rkd,kc->rcd", back_im, sin_w, precision=high)
    ) / (height * width)
    resid = (source + mixed).reshape(rows_here * width, chans)
    totals_two = lax.psum((jnp.sum(resid, axis=-1), jnp.sum(resid * resid, axis=-1)), "col")
    act = (finish_norm(resid, totals_two, width_all) * gain_second).astype(jnp.bfloat16)
    partial_pre = jnp.dot(
        lax.all_gather(act, "row", axis=0, tiled=True), w_in, preferred_element_type=jnp.float32
    )
    summed = lax.psum_scatter(
        partial_pre.astype(jnp.bfloat16), "col", scatter_dimension=0, tiled=True
    ).astype(jnp.float32)
    hidden = jax.nn.gelu(summed + b_in, approximate=False).astype(jnp.bfloat16)
    partial_out = jnp.dot(
        lax.all_gather(hidden, "col", axis=0, tiled=True), w_out, preferred_element_type=jnp.float32
    )
    proj = lax.psum_scatter(
        partial_out.astype(jnp.bfloat16), "row", scatter_dimension=0, tiled=True
    ).astype(jnp.float32)
    result = (resid + proj + b_out).astype(jnp.bfloat16)
    return result.reshape(rows_here, width, chans)


def solution(mesh):
    placed = (
        P("row", None, "col"),
        P(None, None, "row", "col"),
        P("col"),
        P("col"),
        P("col", "row"),
        P("row"),
        P("row", "col"),
        P("col"),
    )
    return jax.shard_map(
        on_device, mesh=mesh, in_specs=placed, out_specs=P("row", None, "col"), check_vma=False
    )
```

profile of v0, /device:TPU:0, one launch (start us, length us, event | category | flops | bytes accessed | tf_op | source)
XLA Modules:
  0.0 433.0 jit_solution(3554515615974507233)
XLA Ops:
  7.9 14.7 %all-reduce.1 = (f32[4,64]{1,0:T(4,128)S(1)}, f32[4,64]{1,0:T(4,128)S(1)}) all-reduce(f32[4,64]{1,0:T(4,128)S(1)} %get-tuple-element.8, f32[4,64]{1,0:T(4,128)S(1)} %get-tuple-element.7), channel_id=1, replica_groups=mesh['row'=16,'col'=8] {'col'}, use_global_device_ids=true, to_apply=%region_3.0 | all-reduce | flops 512 | bytes 4096 | tf_op jit(solution)/shard_map/psum | solution.py:26
  22.6 2.0 fusion.19
  25.6 8.0 %all-to-all-start.1 = ((bf16[4,64,768]{2,0,1:T(4,128)(2,1)}), bf16[4,64,768]{2,0,1:T(4,128)(2,1)S(1)}, u32[]{:S(2)}, u32[]{:S(2)}) async-start(bf16[4,64,768]{2,0,1:T(4,128)(2,1)} %copy.18), calls=%async_computation.1 | async-start | bytes 786432 | tf_op jit(solution)/shard_map/all_to_all | solution.py:36
  35.7 7.3 %all-to-all-done.1 = bf16[4,64,768]{2,0,1:T(4,128)(2,1)S(1)} async-done(((bf16[4,64,768]{2,0,1:T(4,128)(2,1)}), bf16[4,64,768]{2,0,1:T(4,128)(2,1)S(1)}, u32[]{:S(2)}, u32[]{:S(2)}) %all-to-all-start.1) | async-done | bytes 393248 | tf_op jit(solution)/shard_map/all_to_all | solution.py:36
  43.1 3.6 all-to-all-start
  46.6 2.6 fusion.122
  51.2 4.7 %all-to-all-done = bf16[4,64,768]{2,0,1:T(4,128)(2,1)S(1)} async-done(((bf16[4,64,768]{2,0,1:T(4,128)(2,1)}), bf16[4,64,768]{2,0,1:T(4,128)(2,1)S(1)}, u32[]{:S(2)}, u32[]{:S(2)}) %all-to-all-start) | async-done | bytes 393248 | tf_op jit(solution)/shard_map/all_to_all | solution.py:33
  63.6 3.6 all-to-all-start.2
  68.1 2.0 fusion.16
  71.2 5.3 %all-to-all-done.2 = bf16[64,4,768]{2,1,0:T(4,128)(2,1)S(1)} async-done(((bf16[64,4,768]{2,1,0:T(4,128)(2,1)}), bf16[64,4,768]{2,1,0:T(4,128)(2,1)S(1)}, u32[]{:S(2)}, u32[]{:S(2)}) %all-to-all-start.2) | async-done | bytes 393248 | tf_op jit(solution)/shard_map/all_to_all | solution.py:55
  76.5 3.6 all-to-all-start.3
  81.2 1.8 all_to_all.63
  83.0 6.4 %all-to-all-done.3 = bf16[64,4,768]{2,1,0:T(4,128)(2,1)S(1)} async-done(((bf16[64,4,768]{2,1,0:T(4,128)(2,1)}), bf16[64,4,768]{2,1,0:T(4,128)(2,1)S(1)}, u32[]{:S(2)}, u32[]{:S(2)}) %all-to-all-start.3) | async-done | bytes 393248 | tf_op jit(solution)/shard_map/all_to_all | solution.py:58
  90.4 1.6 fusion.47
  92.0 1.8 fusion.121
  94.0 12.4 %all-reduce = (f32[256]{0:T(256)S(1)}, f32[256]{0:T(256)S(1)}) all-reduce(f32[256]{0:T(256)S(1)} %reduce_sum.45, f32[256]{0:T(256)S(1)} %reduce_sum.43), channel_id=1, replica_groups=mesh['row'=16,'col'=8] {'col'}, use_global_device_ids=true, to_apply=%region_7.8 | all-reduce | flops 512 | bytes 4096 | tf_op jit(solution)/shard_map/psum | solution.py:67
  107.4 56.5 %all-gather.3.cloned.1.call-done = bf16[4096,768]{1,0:T(8,128)(2,1)} async-done(((bf16[256,768]{1,0:T(8,128)(2,1)}), bf16[4096,768]{1,0:T(8,128)(2,1)}) %all-gather.3.cloned.1.call-update) | async-done | bytes 6291472 | tf_op jit(solution)/shard_map/all_gather | solution.py:70
  163.9 15.2 %convolution_convert_fusion = bf16[4096,1536]{1,0:T(8,128)(2,1)} fusion(bf16[4096,768]{1,0:T(8,128)(2,1)} %all-gather.3.cloned.1.call-done, bf16[768,1536]{1,0:T(8,128)(2,1)S(1)} %copy-done), kind=kOutput, calls=%fused_computation | convolution fusion | flops 9669967872 | bytes 21233664 | tf_op jit(solution)/shard_map/dot_general | solution.py:69
  179.1 72.0 %reduce-scatter.3.cloned.1.call-done = bf16[512,1536]{1,0:T(8,128)(2,1)} async-done(((bf16[4096,1536]{1,0:T(8,128)(2,1)}), bf16[512,1536]{1,0:T(8,128)(2,1)}) %reduce-scatter.3.cloned.1.call-update) | async-done | bytes 1572880 | tf_op jit(solution)/shard_map/reduce_scatter | solution.py:72
  251.2 8.9 %fusion.2 = bf16[512,1536]{1,0:T(8,128)(2,1)} fusion(bf16[512,1536]{1,0:T(8,128)(2,1)} %reduce-scatter.3.cloned.1.call-done, f32[1536]{0:T(1024)S(1)} %copy-done.6), kind=kLoop, calls=%fused_computation.5 | loop fusion | flops 52690944 | bytes 3151872 | tf_op jit(solution)/shard_map/convert_element_type | solution.py:75
  260.1 67.0 %all-gather.5.cloned.1.call-done = bf16[4096,1536]{1,0:T(8,128)(2,1)} async-done(((bf16[512,1536]{1,0:T(8,128)(2,1)}), bf16[4096,1536]{1,0:T(8,128)(2,1)}) %all-gather.5.cloned.1.call-update) | async-done | bytes 12582928 | tf_op jit(solution)/shard_map/all_gather | solution.py:77
  327.1 15.3 %convolution_convert_fusion.1 = bf16[4096,768]{1,0:T(8,128)(2,1)} fusion(bf16[4096,1536]{1,0:T(8,128)(2,1)} %all-gather.5.cloned.1.call-done, bf16[1536,768]{1,0:T(8,128)(2,1)} %param.14), kind=kOutput, calls=%fused_computation.1 | convolution fusion | flops 9666822144 | bytes 21233664 | tf_op jit(solution)/shard_map/dot_general | solution.py:76
  342.5 82.1 %reduce-scatter.5.cloned.1.call-done = bf16[256,768]{1,0:T(8,128)(2,1)} async-done(((bf16[4096,768]{1,0:T(8,128)(2,1)}), bf16[256,768]{1,0:T(8,128)(2,1)}) %reduce-scatter.5.cloned.1.call-update) | async-done | bytes 393232 | tf_op jit(solution)/shard_map/reduce_scatter | solution.py:79
  424.6 1.9 fusion.27
  (53 shorter events, 19.3 us)
Async XLA Ops:
  6.5 157.3 %copy-start = (bf16[768,1536]{1,0:T(8,128)(2,1)S(1)}, bf16[768,1536]{1,0:T(8,128)(2,1)}, u32[]{:S(2)}) copy-start(bf16[768,1536]{1,0:T(8,128)(2,1)} %param.12) | copy-start | bytes 7077892
  6.5 27.1 %copy-start.4 = (bf16[4,64,768]{2,1,0:T(8,128)(2,1)S(1)}, bf16[4,64,768]{2,1,0:T(8,128)(2,1)}, u32[]{:S(2)}) copy-start(bf16[4,64,768]{2,1,0:T(8,128)(2,1)} %param.8) | copy-start | bytes 1179652
  6.5 27.1 %copy-start.9 = (f32[768]{0:T(1024)S(1)}, f32[768]{0:T(1024)}, u32[]{:S(2)}) copy-start(f32[768]{0:T(1024)} %param.10) | copy-start | bytes 9220
  25.6 17.4 %all-to-all-start.1 = ((bf16[4,64,768]{2,0,1:T(4,128)(2,1)}), bf16[4,64,768]{2,0,1:T(4,128)(2,1)S(1)}, u32[]{:S(2)}, u32[]{:S(2)}) async-start(bf16[4,64,768]{2,0,1:T(4,128)(2,1)} %copy.18), calls=%async_computation.1 | async-start | bytes 786432 | tf_op jit(solution)/shard_map/all_to_all | solution.py:36
  43.1 12.9 %all-to-all-start = ((bf16[4,64,768]{2,0,1:T(4,128)(2,1)}), bf16[4,64,768]{2,0,1:T(4,128)(2,1)S(1)}, u32[]{:S(2)}, u32[]{:S(2)}) async-start(bf16[4,64,768]{2,0,1:T(4,128)(2,1)} %copy.16), calls=%async_computation | async-start | bytes 786432 | tf_op jit(solution)/shard_map/all_to_all | solution.py:33
  58.0 1.8 copy-start.2
  58.0 1.8 copy-start.3
  60.6 0.9 copy-start.1
  63.6 12.9 %all-to-all-start.2 = ((bf16[64,4,768]{2,1,0:T(4,128)(2,1)}), bf16[64,4,768]{2,1,0:T(4,128)(2,1)S(1)}, u32[]{:S(2)}, u32[]{:S(2)}) async-start(bf16[64,4,768]{2,1,0:T(4,128)(2,1)} %copy.21), calls=%async_computation.2 | async-start | bytes 786432 | tf_op jit(solution)/shard_map/all_to_all | solution.py:55
  70.2 21.8 %copy-start.5 = (bf16[4,64,768]{2,1,0:T(8,128)(2,1)S(1)}, bf16[4,64,768]{2,1,0:T(8,128)(2,1)}, u32[]{:S(2)}) copy-start(bf16[4,64,768]{2,1,0:T(8,128)(2,1)} %param.8) | copy-start | bytes 1179652
  76.5 12.9 %all-to-all-start.3 = ((bf16[64,4,768]{2,1,0:T(4,128)(2,1)}), bf16[64,4,768]{2,1,0:T(4,128)(2,1)S(1)}, u32[]{:S(2)}, u32[]{:S(2)}) async-start(bf16[64,4,768]{2,1,0:T(4,128)(2,1)} %copy.23), calls=%async_computation.3 | async-start | bytes 786432 | tf_op jit(solution)/shard_map/all_to_all | solution.py:58
  80.1 83.8 %all-gather.3.cloned.1.call-start = ((), (), s32[]{:S(2)}) async-start(), calls=%async_computation.6 | async-start | bytes 6684672 | tf_op jit(solution)/shard_map/all_gather | solution.py:70
  81.2 25.2 %copy-start.7 = (f32[768]{0:T(1024)S(1)}, f32[768]{0:T(1024)}, u32[]{:S(2)}) copy-start(f32[768]{0:T(1024)} %param.11) | copy-start | bytes 9220
  107.3 143.8 %reduce-scatter.3.cloned.1.call-start = ((), (), s32[]{:S(2)}) async-start(), calls=%async_computation.7 | async-start | bytes 14155776 | tf_op jit(solution)/shard_map/reduce_scatter | solution.py:72
  179.1 72.1 %copy-start.6 = (f32[1536]{0:T(1024)S(1)}, f32[1536]{0:T(1024)}, u32[]{:S(2)}) copy-start(f32[1536]{0:T(1024)} %param.13) | copy-start | bytes 18436
  179.1 148.1 %all-gather.5.cloned.1.call-start = ((), (), s32[]{:S(2)}) async-start(), calls=%async_computation.8 | async-start | bytes 14155776 | tf_op jit(solution)/shard_map/all_gather | solution.py:77
  260.1 164.5 %reduce-scatter.5.cloned.1.call-start = ((), (), s32[]{:S(2)}) async-start(), calls=%async_computation.9 | async-start | bytes 6684672 | tf_op jit(solution)/shard_map/reduce_scatter | solution.py:79
  342.4 82.1 %copy-start.8 = (f32[768]{0:T(1024)S(1)}, f32[768]{0:T(1024)}, u32[]{:S(2)}) copy-start(f32[768]{0:T(1024)} %param.15) | copy-start | bytes 9220
Sparse Core Ops, SparseCore 0:
  107.5 56.3 all-gather.2
  179.2 71.9 reduce-scatter.2
  260.2 66.9 all-gather.4
  342.6 81.9 reduce-scatter.4
where the time goes:
time: 434 us; the launch traced here: 433 us
  waiting for transfers between devices  301 us (69%)
  matrix products  44.3 us (10%)
  blocking collectives  27.1 us (6%)
  starting transfers between devices  19.1 us (4%)
  local copies, waits for them, and re-layouts  14.7 us (3%)
  between operations  13.4 us (3%)
  other arithmetic  13 us (3%)
    reduce_scatter x1, waiting for transfers between devices, on_device(): lax.psum_scatter(partial_out.astype(jnp.bfloat16), 'row', scatter_dimensi...  82.1 us
    reduce_scatter x1, waiting for transfers between devices, on_device(): lax.psum_scatter(partial_pre.astype(jnp.bfloat16), 'col', scatter_dimensi...  72 us
    all_gather x1, waiting for transfers between devices, on_device(): lax.all_gather(hidden, 'col', axis=0, tiled=True)  67 us
    all_gather x1, waiting for transfers between devices, on_device(): lax.all_gather(act, 'row', axis=0, tiled=True)  56.5 us
    dot_general x1, matrix products, on_device(): jnp.dot(lax.all_gather(hidden, 'col', axis=0, tiled=True), w_out, preferr...  15.3 us
    dot_general x1, matrix products, on_device(): jnp.dot(lax.all_gather(act, 'row', axis=0, tiled=True), w_in, preferred_e...  15.2 us
    psum x1, blocking collectives, on_device(): lax.psum((jnp.sum(source, axis=-1), jnp.sum(source * source, axis=-1)), '...  14.7 us
    psum x1, blocking collectives, on_device(): lax.psum((jnp.sum(resid, axis=-1), jnp.sum(resid * resid, axis=-1)), 'col')  12.4 us
  transfers between devices with their start and end apart: 8, of which 8 were waited for; matrix products, arithmetic and copies ran while one was open for 2% of the time, Pallas kernels for 0%

commit v1 on v0

--- a/solution.py
+++ b/solution.py
@@ -74,7 +74,11 @@
     ).astype(jnp.float32)
     hidden = jax.nn.gelu(summed + b_in, approximate=False).astype(jnp.bfloat16)
     partial_out = jnp.dot(
-        lax.all_gather(hidden, "col", axis=0, tiled=True), w_out, preferred_element_type=jnp.float32
+        jnp.concatenate(
+            lax.all_to_all(jnp.stack([hidden] * lax.axis_size("col")), "col", 0, 0), axis=0
+        ),
+        w_out,
+        preferred_element_type=jnp.float32,
     )
     proj = lax.psum_scatter(
         partial_out.astype(jnp.bfloat16), "row", scatter_dimension=0, tiled=True

time: 434 us -> 513 us (1.18)
  blocking collectives: 27.1 us -> 173 us
  waiting for transfers between devices: 301 us -> 233 us
  local copies, waits for them, and re-layouts: 14.7 us -> 20.3 us
    all_to_all x0 -> x1, blocking collectives: none -> 146 us  [on_device(): lax.all_to_all(jnp.stack([hidden] * lax.axis_size('col')), 'col', 0, 0)]
    all_gather x1 -> x0, waiting for transfers between devices: 67 us -> none  [on_device(): lax.all_gather(hidden, 'col', axis=0, tiled=True)]
    another operation x0 -> x1, local copies, waits for them, and re-layouts: none -> 5.6 us  [on_device(): jnp.stack([hidden] * lax.axis_size('col'))]
  transfers between devices with their start and end apart: 8 -> 7, of which waited for: 8 -> 7; matrix products, arithmetic and copies ran while one was open for 2% -> 2% of each run, Pallas kernels for 0% -> 0%
where the time goes in v1:
time: 513 us; the launch traced here: 512 us
  waiting for transfers between devices  233 us (45%)
  blocking collectives  173 us (34%)
  matrix products  40.8 us (8%)
  local copies, waits for them, and re-layouts  20.3 us (4%)
  starting transfers between devices  19 us (4%)
  between operations  13.4 us (3%)
  other arithmetic  12.2 us (2%)
    all_to_all x1, blocking collectives, on_device(): lax.all_to_all(jnp.stack([hidden] * lax.axis_size('col')), 'col', 0, 0)  146 us
    reduce_scatter x1, waiting for transfers between devices, on_device(): lax.psum_scatter(partial_out.astype(jnp.bfloat16), 'row', scatter_dimensi...  81 us
    reduce_scatter x1, waiting for transfers between devices, on_device(): lax.psum_scatter(partial_pre.astype(jnp.bfloat16), 'col', scatter_dimensi...  72 us
    all_gather x1, waiting for transfers between devices, on_device(): lax.all_gather(act, 'row', axis=0, tiled=True)  56.5 us
    dot_general x1, matrix products, on_device(): jnp.dot(lax.all_gather(act, 'row', axis=0, tiled=True), w_in, preferred_e...  15.2 us
    psum x1, blocking collectives, on_device(): lax.psum((jnp.sum(source, axis=-1), jnp.sum(source * source, axis=-1)), '...  14.7 us
    psum x1, blocking collectives, on_device(): lax.psum((jnp.sum(resid, axis=-1), jnp.sum(resid * resid, axis=-1)), 'col')  12.4 us
    dot_general x1, matrix products, on_device(): jnp.dot(jnp.concatenate(lax.all_to_all(jnp.stack([hidden] * lax.axis_size...  11.7 us
  transfers between devices with their start and end apart: 7, of which 7 were waited for; matrix products, arithmetic and copies ran while one was open for 2% of the time, Pallas kernels for 0%

profile of v1, /device:TPU:0, one launch (start us, length us, event | category | flops | bytes accessed | tf_op | source)
XLA Modules:
  0.0 511.7 jit_solution(9821385349188641867)
XLA Ops:
  7.9 14.7 %all-reduce.1 = (f32[4,64]{1,0:T(4,128)S(1)}, f32[4,64]{1,0:T(4,128)S(1)}) all-reduce(f32[4,64]{1,0:T(4,128)S(1)} %get-tuple-element.8, f32[4,64]{1,0:T(4,128)S(1)} %get-tuple-element.7), channel_id=1, replica_groups=mesh['row'=16,'col'=8] {'col'}, use_global_device_ids=true, to_apply=%region_3.0 | all-reduce | flops 512 | bytes 4096 | tf_op jit(solution)/shard_map/psum | solution.py:26
  22.6 2.0 fusion.19
  25.6 8.0 %all-to-all-start.1 = ((bf16[4,64,768]{2,0,1:T(4,128)(2,1)}), bf16[4,64,768]{2,0,1:T(4,128)(2,1)S(1)}, u32[]{:S(2)}, u32[]{:S(2)}) async-start(bf16[4,64,768]{2,0,1:T(4,128)(2,1)} %copy.18), calls=%async_computation.1 | async-start | bytes 786432 | tf_op jit(solution)/shard_map/all_to_all | solution.py:36
  35.7 7.3 %all-to-all-done.1 = bf16[4,64,768]{2,0,1:T(4,128)(2,1)S(1)} async-done(((bf16[4,64,768]{2,0,1:T(4,128)(2,1)}), bf16[4,64,768]{2,0,1:T(4,128)(2,1)S(1)}, u32[]{:S(2)}, u32[]{:S(2)}) %all-to-all-start.1) | async-done | bytes 393248 | tf_op jit(solution)/shard_map/all_to_all | solution.py:36
  43.1 3.6 all-to-all-start
  46.6 2.6 fusion.122
  51.2 4.7 all-to-all-done
  63.6 3.6 all-to-all-start.2
  68.1 2.0 fusion.16
  71.2 5.3 %all-to-all-done.2 = bf16[64,4,768]{2,1,0:T(4,128)(2,1)S(1)} async-done(((bf16[64,4,768]{2,1,0:T(4,128)(2,1)}), bf16[64,4,768]{2,1,0:T(4,128)(2,1)S(1)}, u32[]{:S(2)}, u32[]{:S(2)}) %all-to-all-start.2) | async-done | bytes 393248 | tf_op jit(solution)/shard_map/all_to_all | solution.py:55
  76.5 3.6 all-to-all-start.3
  81.2 1.8 all_to_all.66
  83.0 6.4 %all-to-all-done.3 = bf16[64,4,768]{2,1,0:T(4,128)(2,1)S(1)} async-done(((bf16[64,4,768]{2,1,0:T(4,128)(2,1)}), bf16[64,4,768]{2,1,0:T(4,128)(2,1)S(1)}, u32[]{:S(2)}, u32[]{:S(2)}) %all-to-all-start.3) | async-done | bytes 393248 | tf_op jit(solution)/shard_map/all_to_all | solution.py:58
  92.0 1.8 fusion.121
  94.0 12.4 %all-reduce = (f32[256]{0:T(256)S(1)}, f32[256]{0:T(256)S(1)}) all-reduce(f32[256]{0:T(256)S(1)} %reduce_sum.45, f32[256]{0:T(256)S(1)} %reduce_sum.43), channel_id=1, replica_groups=mesh['row'=16,'col'=8] {'col'}, use_global_device_ids=true, to_apply=%region_7.8 | all-reduce | flops 512 | bytes 4096 | tf_op jit(solution)/shard_map/psum | solution.py:67
  107.4 56.5 %all-gather.2.cloned.1.call-done = bf16[4096,768]{1,0:T(8,128)(2,1)} async-done(((bf16[256,768]{1,0:T(8,128)(2,1)}), bf16[4096,768]{1,0:T(8,128)(2,1)}) %all-gather.2.cloned.1.call-update) | async-done | bytes 6291472 | tf_op jit(solution)/shard_map/all_gather | solution.py:70
  163.9 15.2 %convolution_convert_fusion = bf16[4096,1536]{1,0:T(8,128)(2,1)} fusion(bf16[4096,768]{1,0:T(8,128)(2,1)} %all-gather.2.cloned.1.call-done, bf16[768,1536]{1,0:T(8,128)(2,1)S(1)} %copy-done), kind=kOutput, calls=%fused_computation | convolution fusion | flops 9669967872 | bytes 21233664 | tf_op jit(solution)/shard_map/dot_general | solution.py:69
  179.2 72.0 %reduce-scatter.3.cloned.1.call-done = bf16[512,1536]{1,0:T(8,128)(2,1)} async-done(((bf16[4096,1536]{1,0:T(8,128)(2,1)}), bf16[512,1536]{1,0:T(8,128)(2,1)}) %reduce-scatter.3.cloned.1.call-update) | async-done | bytes 1572880 | tf_op jit(solution)/shard_map/reduce_scatter | solution.py:72
  251.2 8.1 %fusion.2 = bf16[512,1536]{1,0:T(8,128)(2,1)S(1)} fusion(bf16[512,1536]{1,0:T(8,128)(2,1)} %reduce-scatter.3.cloned.1.call-done, f32[1536]{0:T(1024)S(1)} %copy-done.7), kind=kLoop, calls=%fused_computation.5 | loop fusion | flops 52690944 | bytes 3151872 | tf_op jit(solution)/shard_map/convert_element_type | solution.py:75
  259.3 5.6 %stack.2 = bf16[8,512,1536]{2,1,0:T(8,128)(2,1)} broadcast(bf16[512,1536]{1,0:T(8,128)(2,1)S(1)} %fusion.2), dimensions={1,2} | broadcast | bytes 14155776 | tf_op jit(solution)/shard_map/stack | solution.py:78
  264.9 145.7 %all_to_all.77 = bf16[8,512,1536]{2,1,0:T(8,128)(2,1)S(1)} all-to-all(bf16[8,512,1536]{2,1,0:T(8,128)(2,1)} %stack.2), channel_id=1, replica_groups=mesh['row'=16,'col'=8] {'col'}, dimensions={0} | all-to-all | bytes 25165824 | tf_op jit(solution)/shard_map/all_to_all | solution.py:78
  410.6 11.7 %convolution_convert_fusion.1 = bf16[4096,768]{1,0:T(8,128)(2,1)} fusion(bf16[4096,1536]{1,0:T(8,128)(2,1)S(1)} %bitcast.99, bf16[1536,768]{1,0:T(8,128)(2,1)S(1)} %copy-done.10), kind=kOutput, calls=%fused_computation.1 | convolution fusion | flops 9666822144 | bytes 21233664 | tf_op jit(solution)/shard_map/dot_general | solution.py:76
  422.3 81.0 %reduce-scatter.5.cloned.1.call-done = bf16[256,768]{1,0:T(8,128)(2,1)} async-done(((bf16[4096,768]{1,0:T(8,128)(2,1)}), bf16[256,768]{1,0:T(8,128)(2,1)}) %reduce-scatter.5.cloned.1.call-update) | async-done | bytes 393232 | tf_op jit(solution)/shard_map/reduce_scatter | solution.py:83
  503.3 1.9 fusion.27
  (56 shorter events, 20.8 us)
Async XLA Ops:
  6.5 157.3 %copy-start = (bf16[768,1536]{1,0:T(8,128)(2,1)S(1)}, bf16[768,1536]{1,0:T(8,128)(2,1)}, u32[]{:S(2)}) copy-start(bf16[768,1536]{1,0:T(8,128)(2,1)} %param.12) | copy-start | bytes 7077892
  6.5 27.1 %copy-start.5 = (bf16[4,64,768]{2,1,0:T(8,128)(2,1)S(1)}, bf16[4,64,768]{2,1,0:T(8,128)(2,1)}, u32[]{:S(2)}) copy-start(bf16[4,64,768]{2,1,0:T(8,128)(2,1)} %param.8) | copy-start | bytes 1179652
  6.5 27.1 %copy-start.11 = (f32[768]{0:T(1024)S(1)}, f32[768]{0:T(1024)}, u32[]{:S(2)}) copy-start(f32[768]{0:T(1024)} %param.10) | copy-start | bytes 9220
  25.6 17.4 %all-to-all-start.1 = ((bf16[4,64,768]{2,0,1:T(4,128)(2,1)}), bf16[4,64,768]{2,0,1:T(4,128)(2,1)S(1)}, u32[]{:S(2)}, u32[]{:S(2)}) async-start(bf16[4,64,768]{2,0,1:T(4,128)(2,1)} %copy.18), calls=%async_computation.1 | async-start | bytes 786432 | tf_op jit(solution)/shard_map/all_to_all | solution.py:36
  43.1 12.9 %all-to-all-start = ((bf16[4,64,768]{2,0,1:T(4,128)(2,1)}), bf16[4,64,768]{2,0,1:T(4,128)(2,1)S(1)}, u32[]{:S(2)}, u32[]{:S(2)}) async-start(bf16[4,64,768]{2,0,1:T(4,128)(2,1)} %copy.16), calls=%async_computation | async-start | bytes 786432 | tf_op jit(solution)/shard_map/all_to_all | solution.py:33
  58.0 1.8 copy-start.3
  58.0 1.8 copy-start.4
  60.6 0.9 copy-start.2
  63.6 12.9 %all-to-all-start.2 = ((bf16[64,4,768]{2,1,0:T(4,128)(2,1)}), bf16[64,4,768]{2,1,0:T(4,128)(2,1)S(1)}, u32[]{:S(2)}, u32[]{:S(2)}) async-start(bf16[64,4,768]{2,1,0:T(4,128)(2,1)} %copy.21), calls=%async_computation.2 | async-start | bytes 786432 | tf_op jit(solution)/shard_map/all_to_all | solution.py:55
  70.2 21.8 %copy-start.6 = (bf16[4,64,768]{2,1,0:T(8,128)(2,1)S(1)}, bf16[4,64,768]{2,1,0:T(8,128)(2,1)}, u32[]{:S(2)}) copy-start(bf16[4,64,768]{2,1,0:T(8,128)(2,1)} %param.8) | copy-start | bytes 1179652
  76.5 12.9 %all-to-all-start.3 = ((bf16[64,4,768]{2,1,0:T(4,128)(2,1)}), bf16[64,4,768]{2,1,0:T(4,128)(2,1)S(1)}, u32[]{:S(2)}, u32[]{:S(2)}) async-start(bf16[64,4,768]{2,1,0:T(4,128)(2,1)} %copy.23), calls=%async_computation.3 | async-start | bytes 786432 | tf_op jit(solution)/shard_map/all_to_all | solution.py:58
  80.1 83.8 %all-gather.2.cloned.1.call-start = ((), (), s32[]{:S(2)}) async-start(), calls=%async_computation.7 | async-start | bytes 6684672 | tf_op jit(solution)/shard_map/all_gather | solution.py:70
  81.2 25.2 %copy-start.8 = (f32[768]{0:T(1024)S(1)}, f32[768]{0:T(1024)}, u32[]{:S(2)}) copy-start(f32[768]{0:T(1024)} %param.11) | copy-start | bytes 9220
  107.3 143.9 %reduce-scatter.3.cloned.1.call-start = ((), (), s32[]{:S(2)}) async-start(), calls=%async_computation.8 | async-start | bytes 14155776 | tf_op jit(solution)/shard_map/reduce_scatter | solution.py:72
  179.1 72.1 %copy-start.7 = (f32[1536]{0:T(1024)S(1)}, f32[1536]{0:T(1024)}, u32[]{:S(2)}) copy-start(f32[1536]{0:T(1024)} %param.13) | copy-start | bytes 18436
  179.1 324.2 %reduce-scatter.5.cloned.1.call-start = ((), (), s32[]{:S(2)}) async-start(), calls=%async_computation.9 | async-start | bytes 6684672 | tf_op jit(solution)/shard_map/reduce_scatter | solution.py:83
  264.9 145.7 %copy-start.10 = (bf16[1536,768]{1,0:T(8,128)(2,1)S(1)}, bf16[1536,768]{1,0:T(8,128)(2,1)}, u32[]{:S(2)}) copy-start(bf16[1536,768]{1,0:T(8,128)(2,1)} %param.14) | copy-start | bytes 7077892
  422.3 82.9 %copy-start.1 = (bf16[768,1536]{1,0:T(8,128)(2,1)S(1)}, bf16[768,1536]{1,0:T(8,128)(2,1)}, u32[]{:S(2)}) copy-start(bf16[768,1536]{1,0:T(8,128)(2,1)} %param.12) | copy-start | bytes 7077892
  422.3 81.0 %copy-start.9 = (f32[768]{0:T(1024)S(1)}, f32[768]{0:T(1024)}, u32[]{:S(2)}) copy-start(f32[768]{0:T(1024)} %param.15) | copy-start | bytes 9220
Sparse Core Ops, SparseCore 0:
  107.5 56.3 all-gather.1
  179.3 71.9 reduce-scatter.2
  422.5 80.8 reduce-scatter.4
